TPU v7x, 32 devices: a whole 2x2x4 slice. The times are simulated.
32 devices in a mesh: replica: 8 (over z, core), shard: 4 (over y, x).
Axes of the slice: x: 2, y: 2, z: 4, core: 2. Of those that a mesh axis runs over, the one named last changes fastest.
Arguments:
- context_one: bfloat16 [2048, 5120], P('replica', 'shard'), may hold values from -8 to 8
- cotangent_one: bfloat16 [2048, 5120], P('replica', 'shard'), may hold values from -32 to 32
- context_two: bfloat16 [2048, 5120], P('replica', 'shard'), may hold values from -8 to 8
- cotangent_two: bfloat16 [2048, 5120], P('replica', 'shard'), may hold values from -32 to 32
Outputs:
- combined_one: float32 [5120, 5120], P('shard', 'replica')
- combined_two: float32 [5120, 5120], P('shard', 'replica')
All inputs are finite; a program needn't handle non-finite values.
Results may differ from a plain program's by a relative error of at most 0.0047.
Values may be sent and summed in bfloat16 or wider, within the bound.
A program may use at most 128 MiB of HBM per device.

v0:
```python
import jax
import jax.numpy as jnp
from jax import lax
from jax.sharding import PartitionSpec as P

EPSILON = 1e-06


def from_partner(value, axis, stride):
    return lax.ppermute(value, axis, [(i, i ^ 1 << stride) for i in range(lax.axis_size(axis))])


def layer_gradient(context, cotangent):
    tokens = context.shape[0]
    gathered = lax.dot_general(
        context,
        lax.all_gather(cotangent, "shard", axis=1, tiled=True),
        (((0,), (0,)), ((), ())),
        preferred_element_type=jnp.float32,
    )
    return (gathered / float(tokens)).astype(jnp.bfloat16)


def group_total(partial_value, section):
    totals = lax.psum(partial_value, "shard")
    for bit_index in range(section + 1):
        totals = totals + from_partner(totals, "replica", bit_index)
    return totals


def run_sections(carried):
    levels = lax.axis_size("replica").bit_length() - 1
    rep_index = lax.axis_index("replica")
    layer_count = carried.shape[0]
    for section in range(levels):
        my_bit = rep_index >> section & 1
        position = 2 + (levels - 1 - section)
        own_half = lax.dynamic_index_in_dim(carried, my_bit, position, keepdims=False)
        sent_half = lax.dynamic_index_in_dim(carried, 1 - my_bit, position, keepdims=False)
        got_half = from_partner(sent_half, "replica", section)
        own_f = own_half.astype(jnp.float32)
        got_f = got_half.astype(jnp.float32)
        reduce_axes = tuple(range(1, own_f.ndim))
        inner_sum = jnp.sum(own_f * got_f, axis=reduce_axes)
        own_sq = jnp.sum(own_f * own_f, axis=reduce_axes)
        other_sq = jnp.sum(got_f * got_f, axis=reduce_axes)
        lower_sq = jnp.where(my_bit == 0, own_sq, other_sq)
        upper_sq = jnp.where(my_bit == 0, other_sq, own_sq)
        partial_value = jnp.concatenate([inner_sum, lower_sq, upper_sq])
        totals = group_total(partial_value, section)
        inner_total = totals[:layer_count]
        lower_total = totals[layer_count : 2 * layer_count]
        upper_total = totals[2 * layer_count :]
        coeff_lower = 1.0 - inner_total / (2.0 * (lower_total + EPSILON))
        coeff_upper = 1.0 - inner_total / (2.0 * (upper_total + EPSILON))
        own_coeff = jnp.where(my_bit == 0, coeff_lower, coeff_upper)
        other_coeff = jnp.where(my_bit == 0, coeff_upper, coeff_lower)
        bshape = (layer_count,) + (1,) * (own_f.ndim - 1)
        combined = own_coeff.reshape(bshape) * own_f + other_coeff.reshape(bshape) * got_f
        if section == levels - 1:
            carried = combined
        else:
            carried = combined.astype(jnp.bfloat16)
    return carried


def shards(context_one, cotangent_one, context_two, cotangent_two):
    levels = lax.axis_size("replica").bit_length() - 1
    gradients = [
        layer_gradient(context_one, cotangent_one),
        layer_gradient(context_two, cotangent_two),
    ]
    row_count, col_count = gradients[0].shape
    reshaped = [
        grad_block.reshape((1, row_count) + (2,) * levels + (col_count >> levels,))
        for grad_block in gradients
    ]
    first_layer = run_sections(reshaped[0])[0]
    second_layer = run_sections(reshaped[1])[0]
    return (first_layer, second_layer)


def solution(mesh):
    return jax.shard_map(
        shards,
        mesh=mesh,
        in_specs=(
            P("replica", "shard"),
            P("replica", "shard"),
            P("replica", "shard"),
            P("replica", "shard"),
        ),
        out_specs=(P("shard", "replica"), P("shard", "replica")),
        check_vma=False,
    )
```

profile of v0, /device:TPU:0, one launch (start us, length us, event | category | flops | bytes accessed | tf_op | source)
XLA Modules:
  0.0 628.7 jit_solution(14169118106799651605)
XLA Ops:
  7.2 0.7 all-gather.3.cloned.1.call-update
  8.0 0.7 all-gather.5.cloned.1.call-update
  8.7 43.6 %all-gather.3.cloned.1.call-done = bf16[256,5120]{1,0:T(8,128)(2,1)} async-done(((bf16[256,1280]{1,0:T(8,128)(2,1)}), bf16[256,5120]{1,0:T(8,128)(2,1)}) %all-gather.3.cloned.1.call-update) | async-done | bytes 2621456 | tf_op jit(solution)/shard_map/all_gather | solution.py:17
  52.3 8.4 %multiply_convert_fusion.1 = bf16[1280,5120]{1,0:T(8,128)(2,1)} fusion(bf16[256,1280]{1,0:T(8,128)(2,1)S(1)} %copy-done, bf16[256,5120]{1,0:T(8,128)(2,1)} %all-gather.3.cloned.1.call-done), kind=kOutput, calls=%fused_computation.1 | convolution fusion | flops 3368550400 | bytes 16384000 | tf_op jit(solution)/shard_map/dot_general | solution.py:15
  60.7 29.0 %reshape.259 = bf16[1,1280,2,2,2,640]{5,4,3,2,1,0:T(2,128)(2,1)} reshape(bf16[1280,5120]{1,0:T(8,128)(2,1)} %multiply_convert_fusion.1) | data formatting | bytes 26214400 | tf_op jit(solution)/shard_map/reshape | solution.py:75
  89.6 4.1 all-gather.5.cloned.1.call-done
  93.8 8.4 %multiply_convert_fusion = bf16[1280,5120]{1,0:T(8,128)(2,1)} fusion(bf16[256,1280]{1,0:T(8,128)(2,1)S(1)} %copy-done.7, bf16[256,5120]{1,0:T(8,128)(2,1)} %all-gather.5.cloned.1.call-done), kind=kOutput, calls=%fused_computation | convolution fusion | flops 3368550400 | bytes 16384000 | tf_op jit(solution)/shard_map/dot_general | solution.py:15
  102.1 28.9 %reshape.260 = bf16[1,1280,2,2,2,640]{5,4,3,2,1,0:T(2,128)(2,1)} reshape(bf16[1280,5120]{1,0:T(8,128)(2,1)} %multiply_convert_fusion) | data formatting | bytes 26214400 | tf_op jit(solution)/shard_map/reshape | solution.py:75
  131.0 58.1 %constant_dynamic-slice_fusion.1 = (bf16[1,1280,2,2,1,640]{5,4,3,2,1,0:T(2,128)(2,1)}, bf16[1,1280,2,2,1,640]{5,4,3,2,1,0:T(2,128)(2,1)}, bf16[1,1280,2,2,1,640]...) fusion(bf16[1,1280,2,2,2,640]{5,4,3,2,1,0:T(2,128)(2,1)} %reshape.260, s32[]{:T(128)S(6)} %select_n.134, ...), kind=kLoop, calls=%fused_computation.71 | loop fusion | bytes 52428808 | tf_op jit(solution)/shard_map/jit(dynamic_index_in_dim)/dynamic_slice | solution.py:38
  189.1 8.6 %copy.28 = bf16[1,1280,2,2,1,640]{5,1,2,3,4,0:T(8,128)(2,1)} copy(bf16[1,1280,2,2,1,640]{5,4,3,2,1,0:T(2,128)(2,1)} %get-tuple-element.27) | data formatting | bytes 13107200 | tf_op jit(solution)/shard_map/jit(dynamic_index_in_dim)/dynamic_slice | solution.py:39
  197.8 8.5 %copy.29 = bf16[1,1280,2,2,1,640]{5,1,2,3,4,0:T(8,128)(2,1)} copy(bf16[1,1280,2,2,1,640]{5,4,3,2,1,0:T(2,128)(2,1)} %get-tuple-element.48) | data formatting | bytes 13107200 | tf_op jit(solution)/shard_map/jit(dynamic_index_in_dim)/dynamic_slice | solution.py:39
  206.8 1.9 collective-permute-done.9
  208.6 8.9 %fusion.8 = (f32[]{:T(128)}, f32[]{:T(128)}, f32[]{:T(128)}) fusion(bf16[1,1280,2,2,640]{4,1,2,3,0:T(8,128)(2,1)} %collective-permute-done.9, bf16[1,1280,2,2,1,640]{5,4,3,2,1,0:T(2,128)(2,1)} %get-tuple-element.26), kind=kLoop, calls=%fused_computation.20 | loop fusion | flops 26214396 | bytes 13107212 | tf_op jit(solution)/shard_map/reduce_sum | solution.py:44
  220.1 9.0 %fusion.6 = (f32[]{:T(128)}, f32[]{:T(128)}, f32[]{:T(128)}) fusion(bf16[1,1280,2,2,640]{4,1,2,3,0:T(8,128)(2,1)} %collective-permute-done, bf16[1,1280,2,2,1,640]{5,4,3,2,1,0:T(2,128)(2,1)} %get-tuple-element.49), kind=kLoop, calls=%fused_computation.18 | loop fusion | flops 26214396 | bytes 13107212 | tf_op jit(solution)/shard_map/reduce_sum | solution.py:44
  231.6 0.7 pad_maximum_fusion.3
  232.3 0.7 pad_maximum_fusion
  233.1 8.9 %all-reduce.2 = (f32[3]{0:T(128)S(1)}, f32[3]{0:T(128)S(1)}) all-reduce(f32[3]{0:T(128)S(1)} %pad_maximum_fusion, f32[3]{0:T(128)S(1)} %pad_maximum_fusion.3), channel_id=1, replica_groups=mesh['replica'=8,'shard'=4] {'shard'}, use_global_device_ids=true, to_apply=%region_3.4 | all-reduce | flops 6 | bytes 48 | tf_op jit(solution)/shard_map/psum | solution.py:25
  242.5 0.6 collective-permute-done.10
  243.1 0.6 fusion.34
  246.3 0.6 fusion.35
  249.5 10.0 %fusion.5 = bf16[1,1280,2,2,640]{4,1,2,3,0:T(8,128)(2,1)S(1)} fusion(bf16[1,1280,2,2,640]{4,1,2,3,0:T(8,128)(2,1)} %collective-permute-done.9, f32[]{:T(128)} %bitcast.35, f32[]{:T(128)} %bitcast.34, bf16[1,1280,2,2,1,640]{5,4,3,2,1,0:T(2,128)(2,1)} %get-tuple-element.26), kind=kLoop, calls=%fused_computation.17 | loop fusion | flops 19660800 | bytes 19660808 | tf_op jit(solution)/shard_map/convert_element_type | solution.py:63
  259.5 2.2 dynamic-slice_bitcast_fusion
  261.7 1.5 collective-permute-start.11
  263.2 4.9 fusion.2
  268.1 2.2 dynamic-slice_bitcast_fusion.1
  270.3 1.5 copy-done.3
  271.8 1.0 collective-permute-start.2
  272.8 62.9 %collective-permute-done.11 = bf16[1,1280,2,640]{3,1,2,0:T(8,128)(2,1)} collective-permute-done((bf16[1,1280,2,640]{3,1,2,0:T(8,128)(2,1)}, bf16[1,1280,2,640]{3,1,2,0:T(8,128)(2,1)}, u32[]{:S(2)}, u32[]{:S(2)}) %collective-permute-start.11) | collective-permute-done | bytes 3276832 | tf_op jit(solution)/shard_map/ppermute | solution.py:10
  335.7 5.3 fusion.18
  343.5 61.7 %collective-permute-done.2 = bf16[1,1280,2,640]{3,1,2,0:T(8,128)(2,1)} collective-permute-done((bf16[1,1280,2,640]{3,1,2,0:T(8,128)(2,1)}, bf16[1,1280,2,640]{3,1,2,0:T(8,128)(2,1)}, u32[]{:S(2)}, u32[]{:S(2)}) %collective-permute-start.2) | collective-permute-done | bytes 3276832 | tf_op jit(solution)/shard_map/ppermute | solution.py:10
  405.2 4.4 fusion.16
  412.2 0.7 pad_maximum_fusion.4
  412.9 0.7 pad_maximum_fusion.1
  413.6 8.8 %all-reduce.1 = (f32[3]{0:T(128)S(1)}, f32[3]{0:T(128)S(1)}) all-reduce(f32[3]{0:T(128)S(1)} %pad_maximum_fusion.1, f32[3]{0:T(128)S(1)} %pad_maximum_fusion.4), channel_id=1, replica_groups=mesh['replica'=8,'shard'=4] {'shard'}, use_global_device_ids=true, to_apply=%region_7.8 | all-reduce | flops 6 | bytes 48 | tf_op jit(solution)/shard_map/psum | solution.py:25
  423.0 0.6 collective-permute-done.12
  423.6 1.5 collective-permute-start.13
  425.1 0.5 collective-permute-start.4
  425.7 1.5 collective-permute-done.13
  427.2 0.6 fusion.32
  430.4 0.7 fusion.33
  433.8 4.3 fusion.15
  438.1 1.5 dynamic-slice_bitcast_fusion.2
  439.6 2.4 collective-permute-start.14
  442.0 3.2 fusion.12
  445.2 1.5 dynamic-slice_bitcast_fusion.3
  446.7 0.7 copy-done.6
  447.9 101.0 %collective-permute-done.14 = bf16[1,1280,640]{2,1,0:T(8,128)(2,1)} collective-permute-done((bf16[1,1280,640]{2,1,0:T(8,128)(2,1)}, bf16[1,1280,640]{2,1,0:T(8,128)(2,1)}, u32[]{:S(2)}, u32[]{:S(2)}) %collective-permute-start.14) | collective-permute-done | bytes 1638432 | tf_op jit(solution)/shard_map/ppermute | solution.py:10
  548.9 3.4 fusion.28
  554.7 28.1 %collective-permute-done.5 = bf16[1,1280,640]{2,1,0:T(8,128)(2,1)S(1)} collective-permute-done((bf16[1,1280,640]{2,1,0:T(8,128)(2,1)}, bf16[1,1280,640]{2,1,0:T(8,128)(2,1)S(1)}, u32[]{:S(2)}, u32[]{:S(2)}) %collective-permute-start.5) | collective-permute-done | bytes 1638432 | tf_op jit(solution)/shard_map/ppermute | solution.py:10
  582.8 2.9 fusion.26
  588.1 0.7 pad_maximum_fusion.5
  588.8 0.7 pad_maximum_fusion.2
  589.5 8.9 %all-reduce = (f32[3]{0:T(128)S(1)}, f32[3]{0:T(128)S(1)}) all-reduce(f32[3]{0:T(128)S(1)} %pad_maximum_fusion.2, f32[3]{0:T(128)S(1)} %pad_maximum_fusion.5), channel_id=1, replica_groups=mesh['replica'=8,'shard'=4] {'shard'}, use_global_device_ids=true, to_apply=%region_11.12 | all-reduce | flops 6 | bytes 48 | tf_op jit(solution)/shard_map/psum | solution.py:25
  599.0 0.6 collective-permute-done.15
  599.6 0.6 collective-permute-start.16
  600.2 1.4 collective-permute-start.7
  601.6 1.5 collective-permute-done.16
  603.2 1.8 collective-permute-start.17
  605.0 2.0 collective-permute-start.8
  607.0 0.6 collective-permute-done.17
  607.6 0.6 fusion.30
  610.8 0.7 fusion.31
  614.0 4.2 fusion.25
  618.2 3.7 fusion.22
  (58 shorter events, 2.9 us)
Async XLA Ops:
  7.2 45.1 %copy-start = (bf16[256,1280]{1,0:T(8,128)(2,1)S(1)}, bf16[256,1280]{1,0:T(8,128)(2,1)}, u32[]{:S(2)}) copy-start(bf16[256,1280]{1,0:T(8,128)(2,1)} %param.4) | copy-start | bytes 1966084
  7.2 45.1 %all-gather.3.cloned.1.call-start = ((), (), s32[]{:S(2)}) async-start(), calls=%async_computation | async-start | bytes 3276800 | tf_op jit(solution)/shard_map/all_gather | solution.py:17
  7.9 85.9 %all-gather.5.cloned.1.call-start = ((), (), s32[]{:S(2)}) async-start(), calls=%async_computation.1 | async-start | bytes 3276800 | tf_op jit(solution)/shard_map/all_gather | solution.py:17
  60.7 33.1 %copy-start.7 = (bf16[256,1280]{1,0:T(8,128)(2,1)S(1)}, bf16[256,1280]{1,0:T(8,128)(2,1)}, u32[]{:S(2)}) copy-start(bf16[256,1280]{1,0:T(8,128)(2,1)} %param.6) | copy-start | bytes 1966084
  197.8 10.9 %collective-permute-start.9 = (bf16[1,1280,2,2,640]{4,1,2,3,0:T(8,128)(2,1)}, bf16[1,1280,2,2,640]{4,1,2,3,0:T(8,128)(2,1)}, u32[]{:S(2)}, u32[]{:S(2)}) collective-permute-start(bf16[1,1280,2,2,640]{4,1,2,3,0:T(8,128)(2,1)} %bitcast.98), channel_id=1, source_target_pairs={{0,4},{4,0},{8,12},{12,8},{16,20},{20,16},{24,28},{28,24},{1,5},{5... | collective-permute-start | bytes 19660808 | tf_op jit(solution)/shard_map/ppermute | solution.py:10
  206.3 13.8 %collective-permute-start = (bf16[1,1280,2,2,640]{4,1,2,3,0:T(8,128)(2,1)}, bf16[1,1280,2,2,640]{4,1,2,3,0:T(8,128)(2,1)}, u32[]{:S(2)}, u32[]{:S(2)}) collective-permute-start(bf16[1,1280,2,2,640]{4,1,2,3,0:T(8,128)(2,1)} %bitcast.97), channel_id=1, source_target_pairs={{0,4},{4,0},{8,12},{12,8},{16,20},{20,16},{24,28},{28,24},{1,5},{5... | collective-permute-start | bytes 19660808 | tf_op jit(solution)/shard_map/ppermute | solution.py:10
  242.0 1.2 collective-permute-start.10
  242.0 4.3 collective-permute-start.1
  249.5 13.7 %slice-start = ((s8[13107200]{0:T(1024)(128)(4,1)}), s8[4194304]{0:T(1024)(128)(4,1)S(1)}, s32[]{:S(2)}) async-start(s8[13107200]{0:T(1024)(128)(4,1)} %bitcast.93), calls=%async_computation.2 | async-start | bytes 8388608
  249.5 13.7 %slice-start.1 = ((s8[13107200]{0:T(1024)(128)(4,1)}), s8[4194304]{0:T(1024)(128)(4,1)S(1)}, s32[]{:S(2)}) async-start(s8[13107200]{0:T(1024)(128)(4,1)} %bitcast.93), calls=%async_computation.3 | async-start | bytes 8388608
  249.5 13.7 %slice-start.2 = ((s8[13107200]{0:T(1024)(128)(4,1)}), s8[4194304]{0:T(1024)(128)(4,1)S(1)}, s32[]{:S(2)}) async-start(s8[13107200]{0:T(1024)(128)(4,1)} %bitcast.93), calls=%async_computation.4 | async-start | bytes 8388608
  249.5 13.7 %slice-start.3 = ((s8[13107200]{0:T(1024)(128)(4,1)}), s8[524288]{0:T(1024)(128)(4,1)S(1)}, s32[]{:S(2)}) async-start(s8[13107200]{0:T(1024)(128)(4,1)} %bitcast.93), calls=%async_computation.5 | async-start | bytes 1048576
  259.5 8.6 %copy-start.2 = (bf16[1,1280,2,2,640]{4,1,2,3,0:T(8,128)(2,1)}, bf16[1,1280,2,2,640]{4,1,2,3,0:T(8,128)(2,1)S(1)}, u32[]{:S(2)}) copy-start(bf16[1,1280,2,2,640]{4,1,2,3,0:T(8,128)(2,1)S(1)} %fusion.5) | copy-start | bytes 19660804
  261.7 74.1 %collective-permute-start.11 = (bf16[1,1280,2,640]{3,1,2,0:T(8,128)(2,1)}, bf16[1,1280,2,640]{3,1,2,0:T(8,128)(2,1)}, u32[]{:S(2)}, u32[]{:S(2)}) collective-permute-start(bf16[1,1280,2,640]{3,1,2,0:T(8,128)(2,1)} %dynamic-slice_bitcast_fusion), channel_id=1, source_target_pairs={{0,8},{4,12},{8,0},{12,4},{16,24},{20,28},{24,16},{28,20},{1,9},{5... | collective-permute-start | bytes 9830408 | tf_op jit(solution)/shard_map/ppermute | solution.py:10
  268.1 3.7 copy-start.3
  271.8 133.4 %collective-permute-start.2 = (bf16[1,1280,2,640]{3,1,2,0:T(8,128)(2,1)}, bf16[1,1280,2,640]{3,1,2,0:T(8,128)(2,1)}, u32[]{:S(2)}, u32[]{:S(2)}) collective-permute-start(bf16[1,1280,2,640]{3,1,2,0:T(8,128)(2,1)} %dynamic-slice_bitcast_fusion.1), channel_id=1, source_target_pairs={{0,8},{4,12},{8,0},{12,4},{16,24},{20,28},{24,16},{28,20},{1,9},{5... | collective-permute-start | bytes 9830408 | tf_op jit(solution)/shard_map/ppermute | solution.py:10
  272.8 132.4 %copy-start.4 = (bf16[1,1280,2,2,640]{4,1,2,3,0:T(8,128)(2,1)S(1)}, bf16[1,1280,2,2,640]{4,1,2,3,0:T(8,128)(2,1)}, u32[]{:S(2)}) copy-start(bf16[1,1280,2,2,640]{4,1,2,3,0:T(8,128)(2,1)} %copy-done.3) | copy-start | bytes 19660804
  405.2 36.8 %slice-start.4 = ((s8[6553600]{0:T(1024)(128)(4,1)}), s8[2359296]{0:T(1024)(128)(4,1)S(1)}, s32[]{:S(2)}) async-start(s8[6553600]{0:T(1024)(128)(4,1)} %bitcast.95), calls=%async_computation.6 | async-start | bytes 4718592
  422.5 1.2 collective-permute-start.12
  422.5 2.6 collective-permute-start.3
  423.6 3.5 collective-permute-start.13
  425.1 5.3 collective-permute-start.4
  433.8 8.2 %slice-start.5 = ((s8[6553600]{0:T(1024)(128)(4,1)}), s8[4194304]{0:T(1024)(128)(4,1)S(1)}, s32[]{:S(2)}) async-start(s8[6553600]{0:T(1024)(128)(4,1)} %bitcast.95), calls=%async_computation.7 | async-start | bytes 8388608
  438.1 7.1 %copy-start.5 = (bf16[1,1280,2,640]{3,1,2,0:T(8,128)(2,1)}, bf16[1,1280,2,640]{3,1,2,0:T(8,128)(2,1)S(1)}, u32[]{:S(2)}) copy-start(bf16[1,1280,2,640]{3,1,2,0:T(8,128)(2,1)S(1)} %fusion.15) | copy-start | bytes 9830404
  439.6 109.3 %collective-permute-start.14 = (bf16[1,1280,640]{2,1,0:T(8,128)(2,1)}, bf16[1,1280,640]{2,1,0:T(8,128)(2,1)}, u32[]{:S(2)}, u32[]{:S(2)}) collective-permute-start(bf16[1,1280,640]{2,1,0:T(8,128)(2,1)} %dynamic-slice_bitcast_fusion.2), channel_id=1, source_target_pairs={{0,16},{4,20},{8,24},{12,28},{16,0},{20,4},{24,8},{28,12},{1,17},{... | collective-permute-start | bytes 4915208 | tf_op jit(solution)/shard_map/ppermute | solution.py:10
  445.2 2.2 copy-start.6
  447.4 135.4 %collective-permute-start.5 = (bf16[1,1280,640]{2,1,0:T(8,128)(2,1)}, bf16[1,1280,640]{2,1,0:T(8,128)(2,1)S(1)}, u32[]{:S(2)}, u32[]{:S(2)}) collective-permute-start(bf16[1,1280,640]{2,1,0:T(8,128)(2,1)} %dynamic-slice_bitcast_fusion.3), channel_id=1, source_target_pairs={{0,16},{4,20},{8,24},{12,28},{16,0},{20,4},{24,8},{28,12},{1,17},{... | collective-permute-start | bytes 4915208 | tf_op jit(solution)/shard_map/ppermute | solution.py:10
  598.4 1.2 collective-permute-start.15
  598.5 1.7 collective-permute-start.6
  599.6 3.5 collective-permute-start.16
  600.2 4.8 collective-permute-start.7
  603.2 4.4 collective-permute-start.17
  605.0 5.8 collective-permute-start.8
  614.0 7.9 %copy-start.1 = (bf16[256,1280]{1,0:T(8,128)(2,1)S(1)}, bf16[256,1280]{1,0:T(8,128)(2,1)}, u32[]{:S(2)}) copy-start(bf16[256,1280]{1,0:T(8,128)(2,1)} %param.4) | copy-start | bytes 1966084
Sparse Core Ops, SparseCore 0:
  9.9 42.3 all-gather.2
  54.1 39.6 all-gather.4
where the time goes:
time: 631 us; the launch traced here: 629 us
  waiting for transfers between devices  310 us (49%)
  local copies, waits for them, and re-layouts  146 us (23%)
  other arithmetic  68.5 us (11%)
  between operations  44.7 us (7%)
  blocking collectives  26.6 us (4%)
  matrix products  16.8 us (3%)
  starting transfers between devices  15.5 us (2%)
    ppermute x18, waiting for transfers between devices, from_partner(): lax.ppermute(value, axis, [(i, i ^ 1 << stride) for i in range(lax.axis_s...  261 us
    dynamic_slice x1, local copies, waits for them, and re-layouts, run_sections(): lax.dynamic_index_in_dim(carried, my_bit, position, keepdims=False)  58.1 us
    reshape x2, local copies, waits for them, and re-layouts, shards(): grad_block.reshape((1, row_count) + (2,) * levels + (col_count >> levels,))  57.8 us
    all_gather x2, waiting for transfers between devices, layer_gradient(): lax.all_gather(cotangent, 'shard', axis=1, tiled=True)  47.7 us
    reduce_sum x6, other arithmetic, run_sections(): inner_sum = jnp.sum(own_f * got_f, axis=reduce_axes)  33.9 us
    psum x3, blocking collectives, group_total(): totals = lax.psum(partial_value, 'shard')  26.6 us
    convert_element_type x4, other arithmetic, run_sections(): carried = combined.astype(jnp.bfloat16)  22.4 us
    dynamic_slice x2, local copies, waits for them, and re-layouts, run_sections(): lax.dynamic_index_in_dim(carried, 1 - my_bit, position, keepdims=False)  17.1 us
  transfers between devices with their start and end apart: 20, of which 13 were waited for; matrix products, arithmetic and copies ran while one was open for 12% of the time, Pallas kernels for 0%

commit v1 on v0

v1 whole, which is shorter than its diff:
```python
import functools

import jax
import jax.numpy as jnp
from jax import lax
from jax.experimental import pallas as pl
from jax.experimental.pallas import tpu as pltpu
from jax.sharding import PartitionSpec as P

EPSILON = 1e-06
MESH = pl.DeviceIdType.MESH
LAYERS = 2
LANES = 128
F32 = jnp.float32


def pair_coefficient(inner, own_sq, other_sq):
    own_sq = jnp.maximum(own_sq, 0.0)
    bound = jnp.sqrt(own_sq) * jnp.sqrt(jnp.maximum(other_sq, 0.0))
    inner = jnp.clip(inner, -bound, bound)
    return 1.0 - inner / (2.0 * (own_sq + EPSILON))


def replica_weights(gram, n):
    row = lax.broadcasted_iota(jnp.int32, gram.shape, 0)
    lane = lax.broadcasted_iota(jnp.int32, gram.shape, 1)
    col_w = jnp.ones((n, 1), F32)
    row_w = jnp.ones((1, LANES), F32)
    for level in range(n.bit_length() - 1):
        same = (row >> level) == (lane >> level)
        other = (row >> level) == ((lane >> level) ^ 1)
        scaled = gram * col_w * row_w
        inside = jnp.where(same, scaled, 0.0)
        across = jnp.where(other, scaled, 0.0)
        in_row = jnp.sum(inside, axis=0, keepdims=True)
        ac_row = jnp.sum(across, axis=0, keepdims=True)
        in_col = jnp.sum(inside, axis=1, keepdims=True)
        ac_col = jnp.sum(across, axis=1, keepdims=True)

        def total(mask, value, axis):
            return jnp.sum(jnp.where(mask, value, 0.0), axis=axis, keepdims=True)

        col_w = col_w * pair_coefficient(
            total(same, ac_row, 1), total(same, in_row, 1), total(other, in_row, 1)
        )
        row_w = row_w * pair_coefficient(
            total(same, ac_col, 0), total(same, in_col, 0), total(other, in_col, 0)
        )
    return col_w


def kernel(
    n, ns, tok, cols, ocols, mt,
    c1, t1, c2, t2, out1, out2,
    c_all, t_all, stage, t_scaled, obuf, acc, ar1, ar2, mine,
    loc_sem, tl_sem, ta_send, ta_recv, tb_loc, tb_send, tb_recv, tc_send, tc_recv,
    c_send, c_recv, sib_send, sib_recv, a1_send, a1_recv, a2_send, a2_recv, osem,
):
    nz = n // 2
    tq = tok // ns
    c_in, t_in, outs = (c1, c2), (t1, t2), (out1, out2)
    r = lax.axis_index("replica")
    s = lax.axis_index("shard")
    z = r // 2
    core = r % 2
    sib = z * 2 + 1 - core
    layers = range(LAYERS)

    def remote(src, dst, ss, rs, dr, ds):
        return pltpu.make_async_remote_copy(
            src_ref=src, dst_ref=dst, send_sem=ss, recv_sem=rs,
            device_id=(dr, ds), device_id_type=MESH,
        )

    def rows(rep):
        return pl.ds(pl.multiple_of(rep * tok, tok), tok)

    def quarter(q):
        return pl.ds(pl.multiple_of(q * tq, tq), tq)

    def t_half(l, q, h):
        if ocols % LANES == 0:
            return t_in[l].at[quarter(q), pl.ds(h * ocols, ocols)]
        return t_in[l].at[h, quarter(q)]

    barrier = pltpu.get_barrier_semaphore()
    for q in range(ns):
        @pl.when(q != s)
        def _():
            pl.semaphore_signal(barrier, inc=1, device_id=(r, q), device_id_type=MESH)
    for rep in range(n):
        @pl.when(rep != r)
        def _():
            pl.semaphore_signal(barrier, inc=1, device_id=(rep, s), device_id_type=MESH)
    local = []
    for l in layers:
        local.append(pltpu.make_async_copy(c_in[l], c_all.at[l, rows(r)], loc_sem.at[l]))
        for h in range(2):
            local.append(pltpu.make_async_copy(t_half(l, s, h), stage.at[l, s, h], tl_sem.at[l, h]))
    for copy in local:
        copy.start()
    pl.semaphore_wait(barrier, n + ns - 2)

    def ta(l, q, h):
        return remote(t_half(l, q, h), stage.at[l, s, h], ta_send.at[l, q, h],
                      ta_recv.at[l, s, h], r, q)

    def ta_in(l, q, h):
        return remote(t_half(l, s, h), stage.at[l, q, h], ta_send.at[l, q, h],
                      ta_recv.at[l, q, h], r, q)

    def tb(l, j):
        return remote(stage.at[l, j // 2, j % 2], t_all.at[l, r, quarter(s)],
                      tb_send.at[l, j], tb_recv.at[l, r], j, s)

    def tb_in(l, j):
        return remote(stage.at[l, j // 2, j % 2], t_all.at[l, j, quarter(s)],
                      tb_send.at[l, j], tb_recv.at[l, j], j, s)

    def tb_own(l, j):
        return pltpu.make_async_copy(stage.at[l, j // 2, j % 2], t_all.at[l, r, quarter(s)], tb_loc.at[l])

    def tc(l, q):
        part = t_all.at[l, :, quarter(s)]
        return remote(part, part, tc_send.at[l, q], tc_recv.at[l, s], r, q)

    def tc_in(l, q):
        part = t_all.at[l, :, quarter(q)]
        return remote(part, part, tc_send.at[l, q], tc_recv.at[l, q], r, q)

    def c_copy(l, way, t):
        chip = z - t if way == 0 else z + t
        block = c_all.at[l, rows(2 * chip + core)]
        src = c_in[l] if t == 0 else block
        to = r + 2 if way == 0 else r - 2
        return remote(src, block, c_send.at[l, way, t], c_recv.at[l, way, t], to, s)

    def c_sends(way, t):
        if way == 0:
            return jnp.logical_and(z < nz - 1, z - t >= 0)
        return jnp.logical_and(z > 0, z + t <= nz - 1)

    def c_in_chip(way, t):
        return z - 1 - t if way == 0 else z + 1 + t

    def c_valid(way, t):
        chip = c_in_chip(way, t)
        return chip >= 0 if way == 0 else chip <= nz - 1

    def c_wait(l, way, t):
        block = c_all.at[l, rows(2 * c_in_chip(way, t) + core)]
        remote(block, block, c_send.at[l, way, t], c_recv.at[l, way, t], sib, s).wait_recv()

    def sib_out(l, chip):
        block = c_all.at[l, rows(2 * chip + core)]
        return remote(block, block, sib_send.at[l, chip], sib_recv.at[l, chip], sib, s)

    def sib_in(l, chip):
        block = c_all.at[l, rows(2 * chip + 1 - core)]
        return remote(block, block, sib_send.at[l, chip], sib_recv.at[l, chip], sib, s)

    def when_each(pairs):
        for cond, fn in pairs:
            pl.when(cond)(fn)

    for l in layers:
        for q in range(ns):
            for h in range(2):
                when_each([(q != s, lambda l=l, q=q, h=h: ta(l, q, h).start())])
        for way in range(2):
            when_each([(c_sends(way, 0), lambda l=l, way=way: c_copy(l, way, 0).start())])
    for copy in local:
        copy.wait()
    for l in layers:
        sib_out(l, z).start()

    for l in layers:
        for q in range(ns):
            for h in range(2):
                when_each([(q != s, lambda l=l, q=q, h=h: ta_in(l, q, h).wait_recv())])
        for j in range(n):
            when_each([
                (j != r, lambda l=l, j=j: tb(l, j).start()),
                (j == r, lambda l=l, j=j: tb_own(l, j).start()),
            ])

    def arrive(l, t):
        for way in range(2):
            def take(l=l, way=way, t=t):
                c_wait(l, way, t)
                if t + 1 <= nz - 2:
                    when_each([(c_sends(way, t + 1), lambda: c_copy(l, way, t + 1).start())])
                sib_out(l, c_in_chip(way, t)).start()

            when_each([(c_valid(way, t), take)])

    def share_t(l):
        for j in range(n):
            when_each([
                (j != r, lambda l=l, j=j: tb_in(l, j).wait_recv()),
                (j == r, lambda l=l, j=j: tb_own(l, j).wait()),
            ])
        for q in range(ns):
            when_each([(q != s, lambda l=l, q=q: tc(l, q).start())])

    for t in range(max(nz - 2, 1)):
        for l in layers:
            arrive(l, t)
            if t == 0:
                share_t(l)

    def gram_block(l, i, j):
        a = pl.ds(pl.multiple_of(i * 2 * tok, 2 * tok), 2 * tok)
        b = pl.ds(pl.multiple_of(j * 2 * tok, 2 * tok), 2 * tok)
        dims = (((1,), (1,)), ((), ()))
        x = lax.dot_general(c_all[l, a, :], c_all[l, b, :], dims, preferred_element_type=F32)
        ti = t_all[l, pl.ds(2 * i, 2)].reshape(2 * tok, ocols)
        tj = t_all[l, pl.ds(2 * j, 2)].reshape(2 * tok, ocols)
        y = lax.dot_general(ti, tj, dims, preferred_element_type=F32)
        p = x * y
        for da in range(2):
            part = jnp.sum(p[da * tok : (da + 1) * tok], axis=0, keepdims=True)
            for db in range(2):
                v = part[:, db * tok : db * tok + LANES]
                for e in range(1, tok // LANES):
                    v = v + part[:, db * tok + e * LANES : db * tok + (e + 1) * LANES]
                acc[l, 2 * i + da, pl.ds(2 * j + db, 1), :] = v
                acc[l, 2 * j + db, pl.ds(2 * i + da, 1), :] = v

    def gram_step(l, t):
        for way in range(2):
            when_each([(c_valid(way, t), lambda l=l, way=way, t=t: sib_in(l, c_in_chip(way, t)).wait_recv())])
        lo0, hi0 = jnp.maximum(z - t, 0), jnp.minimum(z + t, nz - 1)
        lo1, hi1 = jnp.maximum(z - 1 - t, 0), jnp.minimum(z + 1 + t, nz - 1)
        down = jnp.where(lo1 < lo0, hi0 - lo1 + 1, 0)
        up = jnp.where(hi1 > hi0, hi1 - lo1 + 1, 0)
        own = 1 if t == 0 else 0

        def body(k, _):
            i = jnp.where(k < own, z, jnp.where(k < own + down, lo1, lo1 + k - own - down))
            j = jnp.where(k < own, z, jnp.where(k < own + down, lo1 + k - own, hi1))
            gram_block(l, i, j)
            return 0

        lax.fori_loop(0, own + down + up, body, 0)

    def all_sum(l, value):
        ar1[l, s] = value
        mine[l, 0] = value
        for q in range(ns):
            when_each([(q != s, lambda q=q: remote(
                mine.at[l, 0], ar1.at[l, s], a1_send.at[l, q], a1_recv.at[l, s], r, q).start())])
        for q in range(ns):
            when_each([(q != s, lambda q=q: remote(
                mine.at[l, 0], ar1.at[l, q], a1_send.at[l, q], a1_recv.at[l, q], r, q).wait_recv())])
        value = jnp.sum(ar1[l], axis=0)
        ar2[l, r] = value
        mine[l, 1] = value
        for j in range(n):
            when_each([(j != r, lambda j=j: remote(
                mine.at[l, 1], ar2.at[l, r], a2_send.at[l, j], a2_recv.at[l, r], j, s).start())])
        for j in range(n):
            when_each([(j != r, lambda j=j: remote(
                mine.at[l, 1], ar2.at[l, j], a2_send.at[l, j], a2_recv.at[l, j], j, s).wait_recv())])
        return jnp.sum(ar2[l], axis=0)

    def out_copy(l, m):
        part = pl.ds(pl.multiple_of(m * mt, mt), mt)
        return pltpu.make_async_copy(obuf.at[l, part], outs[l].at[part], osem.at[l, m])

    def finish(l):
        lane = lax.broadcasted_iota(jnp.int32, (n, LANES), 1)
        gram = jnp.zeros((n, LANES), F32)
        for a in range(n):
            gram = jnp.where(lane == a, jnp.sum(acc[l, a], axis=1, keepdims=True), gram)
        gram = all_sum(l, gram) * (1.0 / (float(tok) * float(tok)))
        weights = replica_weights(gram, n) * (1.0 / float(tok))
        for rep in range(n):
            w = jnp.broadcast_to(weights[rep : rep + 1, :], (tok, ocols))
            t_scaled[rep * tok : (rep + 1) * tok, :] = (t_all[l, rep].astype(F32) * w).astype(jnp.bfloat16)

        def body(m, _):
            part = pl.ds(pl.multiple_of(m * mt, mt), mt)
            obuf[l, part, :] = lax.dot_general(
                c_all[l, :, part] if mt != cols else c_all[l],
                t_scaled[...], (((0,), (0,)), ((), ())), preferred_element_type=F32,
            )
            out_copy(l, m).start()
            return 0

        lax.fori_loop(0, cols // mt, body, 0)

    for l in layers:
        sib_in(l, z).wait_recv()
        for q in range(ns):
            when_each([(q != s, lambda l=l, q=q: tc_in(l, q).wait_recv())])
        for t in range(nz - 1):
            if t == nz - 2 and t > 0:
                arrive(l, t)
            gram_step(l, t)
        finish(l)

    for l in layers:
        for q in range(ns):
            def drain(l=l, q=q):
                for h in range(2):
                    ta(l, q, h).wait_send()
                tc(l, q).wait_send()
                remote(mine.at[l, 0], ar1.at[l, s], a1_send.at[l, q], a1_recv.at[l, s], r, q).wait_send()

            when_each([(q != s, drain)])
        for j in range(n):
            def drain_b(l=l, j=j):
                tb(l, j).wait_send()
                remote(mine.at[l, 1], ar2.at[l, r], a2_send.at[l, j], a2_recv.at[l, r], j, s).wait_send()

            when_each([(j != r, drain_b)])
        sib_out(l, z).wait_send()
        for t in range(nz - 1):
            for way in range(2):
                when_each([
                    (c_sends(way, t), lambda l=l, way=way, t=t: c_copy(l, way, t).wait_send()),
                    (c_valid(way, t), lambda l=l, way=way, t=t: sib_out(l, c_in_chip(way, t)).wait_send()),
                ])
        for m in range(cols // mt):
            out_copy(l, m).wait()


def solution(mesh):
    n, ns = mesh.shape["replica"], mesh.shape["shard"]

    def shards(context_one, cotangent_one, context_two, cotangent_two):
        tok, cols = context_one.shape
        ocols = cols * ns // n
        mt = 256 if cols % 256 == 0 else cols
        nz = n // 2

        def halves(t):
            if ocols % LANES == 0:
                return t
            return t.reshape(tok, 2, ocols).transpose(1, 0, 2)

        dma = lambda *shape: pltpu.SemaphoreType.DMA(shape)
        bf = jnp.bfloat16
        any_spec = pl.BlockSpec(memory_space=pl.ANY)
        flops = LAYERS * 2 * n * tok * (cols * ocols + n * tok * (cols + ocols) // 2)
        return pl.pallas_call(
            functools.partial(kernel, n, ns, tok, cols, ocols, mt),
            out_shape=[jax.ShapeDtypeStruct((cols, ocols), F32)] * 2,
            in_specs=[any_spec] * 4,
            out_specs=[any_spec] * 2,
            scratch_shapes=[
                pltpu.VMEM((LAYERS, n * tok, cols), bf),
                pltpu.VMEM((LAYERS, n, tok, ocols), bf),
                pltpu.VMEM((LAYERS, ns, 2, tok // ns, ocols), bf),
                pltpu.VMEM((n * tok, ocols), bf),
                pltpu.VMEM((LAYERS, cols, ocols), F32),
                pltpu.VMEM((LAYERS, n, n, LANES), F32),
                pltpu.VMEM((LAYERS, ns, n, LANES), F32),
                pltpu.VMEM((LAYERS, n, n, LANES), F32),
                pltpu.VMEM((LAYERS, 2, n, LANES), F32),
                dma(LAYERS), dma(LAYERS, 2),
                dma(LAYERS, ns, 2), dma(LAYERS, ns, 2),
                dma(LAYERS), dma(LAYERS, n), dma(LAYERS, n),
                dma(LAYERS, ns), dma(LAYERS, ns),
                dma(LAYERS, 2, nz), dma(LAYERS, 2, nz),
                dma(LAYERS, nz), dma(LAYERS, nz),
                dma(LAYERS, ns), dma(LAYERS, ns),
                dma(LAYERS, n), dma(LAYERS, n),
                dma(LAYERS, cols // mt),
            ],
            compiler_params=pltpu.CompilerParams(
                collective_id=0, has_side_effects=True, vmem_limit_bytes=56 * 2**20
            ),
            cost_estimate=pl.CostEstimate(
                flops=flops, transcendentals=0,
                bytes_accessed=LAYERS * (2 * tok * cols * 2 + cols * ocols * 4),
            ),
        )(context_one, halves(cotangent_one), context_two, halves(cotangent_two))

    return jax.shard_map(
        shards,
        mesh=mesh,
        in_specs=(P("replica", "shard"),) * 4,
        out_specs=(P("shard", "replica"),) * 2,
        check_vma=False,
    )
```

time: 631 us -> 160 us (0.25)
  waiting for transfers between devices: 310 us -> 0 us
  Pallas kernels: 0 us -> 153 us
  local copies, waits for them, and re-layouts: 146 us -> 5.71 us
  other arithmetic: 68.5 us -> 0 us
  between operations: 44.7 us -> 0.65 us
  blocking collectives: 26.6 us -> 0 us
  matrix products: 16.8 us -> 0 us
  starting transfers between devices: 15.5 us -> 0 us
    ppermute x18 -> x0, waiting for transfers between devices: 261 us -> none  [from_partner(): lax.ppermute(value, axis, [(i, i ^ 1 << stride) for i in range(lax.axis_s...]
    pallas_call x0 -> x1, Pallas kernels: none -> 153 us  [shards(): pl.pallas_call(functools.partial(kernel, n, ns, tok, cols, ocols, mt), ou...]
    dynamic_slice x3 -> x0, local copies, waits for them, and re-layouts: 75.3 us -> none  [the longest x1 58.1 us: run_sections(): lax.dynamic_index_in_dim(carried, my_bit, position, keepdims=False)]
    reshape x2 -> x0, local copies, waits for them, and re-layouts: 57.8 us -> none  [shards(): grad_block.reshape((1, row_count) + (2,) * levels + (col_count >> levels,))]
    all_gather x2 -> x0, waiting for transfers between devices: 47.7 us -> none  [layer_gradient(): lax.all_gather(cotangent, 'shard', axis=1, tiled=True)]
    reduce_sum x6 -> x0, other arithmetic: 33.9 us -> none  [run_sections(): inner_sum = jnp.sum(own_f * got_f, axis=reduce_axes)]
    psum x3 -> x0, blocking collectives: 26.6 us -> none  [group_total(): totals = lax.psum(partial_value, 'shard')]
    convert_element_type x4 -> x0, other arithmetic: 22.4 us -> none  [run_sections(): carried = combined.astype(jnp.bfloat16)]
  transfers between devices with their start and end apart: 20 -> 0, of which waited for: 13 -> 0; matrix products, arithmetic and copies ran while one was open for 12% -> 0% of each run, Pallas kernels for 0% -> 0%
where the time goes in v1:
time: 160 us
  Pallas kernels  153 us (96%)
  local copies, waits for them, and re-layouts  5.71 us (4%)
    pallas_call x1, Pallas kernels, shards(): pl.pallas_call(functools.partial(kernel, n, ns, tok, cols, ocols, mt), ou...  153 us
    unnamed x4, local copies, waits for them, and re-layouts  5.71 us

profile of v1, /device:TPU:0, one launch (start us, length us, event | category | flops | bytes accessed | tf_op | source)
XLA Modules:
  0.0 159.6 jit_solution(10238946147282850924)
XLA Ops:
  0.6 153.2 %shard_map.59 = (f32[1280,640]{1,0:T(8,128)}, f32[1280,640]{1,0:T(8,128)}) custom-call(bf16[256,1280]{1,0:T(8,128)(2,1)} %c1.1, bf16[256,1280]{1,0:T(8,128)(2,1)} %t1.1, bf16[256,1280]{1,0:T(8,128)(2,1)} %c2.1, bf16[256,1280]{1,0:T(8,128)(2,1)} %t2.1), custom_call_target="tpu_custom_call" | custom-call | flops 22817013760 | bytes 9175040 | tf_op jit(solution)/shard_map/pallas_call | solution.py:347
  153.9 0.0 copy-start
  153.9 4.0 %copy.8 = f32[1280,640]{1,0:T(8,128)} copy(f32[1280,640]{1,0:T(8,128)} %get-tuple-element.4) | data formatting | bytes 6553600
  157.9 0.0 copy-done
  157.9 1.7 %copy.9 = f32[1280,640]{1,0:T(8,128)} copy(f32[1280,640]{1,0:T(8,128)S(1)} %copy-done) | data formatting | bytes 6553600
Async XLA Ops:
  153.9 4.0 %copy-start = (f32[1280,640]{1,0:T(8,128)S(1)}, f32[1280,640]{1,0:T(8,128)}, u32[]{:S(2)}) copy-start(f32[1280,640]{1,0:T(8,128)} %get-tuple-element.5) | copy-start | bytes 9830404

commit v2 on v1

--- a/solution.py
+++ b/solution.py
@@ -163,25 +163,27 @@
         for cond, fn in pairs:
             pl.when(cond)(fn)
 
-    for l in layers:
+    def ta_start(l):
         for q in range(ns):
             for h in range(2):
-                when_each([(q != s, lambda l=l, q=q, h=h: ta(l, q, h).start())])
+                when_each([(q != s, lambda q=q, h=h: ta(l, q, h).start())])
+
+    def own_start(l):
         for way in range(2):
-            when_each([(c_sends(way, 0), lambda l=l, way=way: c_copy(l, way, 0).start())])
-    for copy in local:
-        copy.wait()
-    for l in layers:
-        sib_out(l, z).start()
-
-    for l in layers:
+            when_each([(c_sends(way, 0), lambda way=way: c_copy(l, way, 0).start())])
+
+    def own_sent(l):
+        for way in range(2):
+            when_each([(c_sends(way, 0), lambda way=way: c_copy(l, way, 0).wait_send())])
+
+    def tb_start(l):
         for q in range(ns):
             for h in range(2):
-                when_each([(q != s, lambda l=l, q=q, h=h: ta_in(l, q, h).wait_recv())])
+                when_each([(q != s, lambda q=q, h=h: ta_in(l, q, h).wait_recv())])
         for j in range(n):
             when_each([
-                (j != r, lambda l=l, j=j: tb(l, j).start()),
-                (j == r, lambda l=l, j=j: tb_own(l, j).start()),
+                (j != r, lambda j=j: tb(l, j).start()),
+                (j == r, lambda j=j: tb_own(l, j).start()),
             ])
 
     def arrive(l, t):
@@ -202,12 +204,6 @@
             ])
         for q in range(ns):
             when_each([(q != s, lambda l=l, q=q: tc(l, q).start())])
-
-    for t in range(max(nz - 2, 1)):
-        for l in layers:
-            arrive(l, t)
-            if t == 0:
-                share_t(l)
 
     def gram_block(l, i, j):
         a = pl.ds(pl.multiple_of(i * 2 * tok, 2 * tok), 2 * tok)
@@ -244,12 +240,18 @@
 
         lax.fori_loop(0, own + down + up, body, 0)
 
-    def all_sum(l, value):
+    def rows_sum_start(l):
+        lane = lax.broadcasted_iota(jnp.int32, (n, LANES), 1)
+        value = jnp.zeros((n, LANES), F32)
+        for a in range(n):
+            value = jnp.where(lane == a, jnp.sum(acc[l, a], axis=1, keepdims=True), value)
         ar1[l, s] = value
         mine[l, 0] = value
         for q in range(ns):
             when_each([(q != s, lambda q=q: remote(
                 mine.at[l, 0], ar1.at[l, s], a1_send.at[l, q], a1_recv.at[l, s], r, q).start())])
+
+    def replica_sum_start(l):
         for q in range(ns):
             when_each([(q != s, lambda q=q: remote(
                 mine.at[l, 0], ar1.at[l, q], a1_send.at[l, q], a1_recv.at[l, q], r, q).wait_recv())])
@@ -259,6 +261,8 @@
         for j in range(n):
             when_each([(j != r, lambda j=j: remote(
                 mine.at[l, 1], ar2.at[l, r], a2_send.at[l, j], a2_recv.at[l, r], j, s).start())])
+
+    def gram_total(l):
         for j in range(n):
             when_each([(j != r, lambda j=j: remote(
                 mine.at[l, 1], ar2.at[l, j], a2_send.at[l, j], a2_recv.at[l, j], j, s).wait_recv())])
@@ -269,11 +273,7 @@
         return pltpu.make_async_copy(obuf.at[l, part], outs[l].at[part], osem.at[l, m])
 
     def finish(l):
-        lane = lax.broadcasted_iota(jnp.int32, (n, LANES), 1)
-        gram = jnp.zeros((n, LANES), F32)
-        for a in range(n):
-            gram = jnp.where(lane == a, jnp.sum(acc[l, a], axis=1, keepdims=True), gram)
-        gram = all_sum(l, gram) * (1.0 / (float(tok) * float(tok)))
+        gram = gram_total(l) * (1.0 / (float(tok) * float(tok)))
         weights = replica_weights(gram, n) * (1.0 / float(tok))
         for rep in range(n):
             w = jnp.broadcast_to(weights[rep : rep + 1, :], (tok, ocols))
@@ -290,15 +290,48 @@
 
         lax.fori_loop(0, cols // mt, body, 0)
 
+    def inputs_ready(l):
+        sib_in(l, z).wait_recv()
+        for q in range(ns):
+            when_each([(q != s, lambda q=q: tc_in(l, q).wait_recv())])
+
+    last = nz - 2
+    ta_start(0)
+    own_start(0)
+    ta_start(1)
+    for copy in local:
+        copy.wait()
     for l in layers:
-        sib_in(l, z).wait_recv()
-        for q in range(ns):
-            when_each([(q != s, lambda l=l, q=q: tc_in(l, q).wait_recv())])
-        for t in range(nz - 1):
-            if t == nz - 2 and t > 0:
-                arrive(l, t)
-            gram_step(l, t)
-        finish(l)
+        sib_out(l, z).start()
+    tb_start(0)
+    own_sent(0)
+    own_start(1)
+    arrive(0, 0)
+    tb_start(1)
+    share_t(0)
+    for t in range(1, last):
+        arrive(0, t)
+        arrive(1, t - 1)
+        if t == 1:
+            share_t(1)
+    inputs_ready(0)
+    for t in range(last):
+        gram_step(0, t)
+    arrive(1, last - 1)
+    arrive(0, last)
+    gram_step(0, last)
+    rows_sum_start(0)
+    inputs_ready(1)
+    gram_step(1, 0)
+    replica_sum_start(0)
+    for t in range(1, last):
+        gram_step(1, t)
+    finish(0)
+    arrive(1, last)
+    gram_step(1, last)
+    rows_sum_start(1)
+    replica_sum_start(1)
+    finish(1)
 
     for l in layers:
         for q in range(ns):
@@ -319,7 +352,7 @@
         for t in range(nz - 1):
             for way in range(2):
                 when_each([
-                    (c_sends(way, t), lambda l=l, way=way, t=t: c_copy(l, way, t).wait_send()),
+                    (jnp.logical_and(c_sends(way, t), l + t > 0), lambda l=l, way=way, t=t: c_copy(l, way, t).wait_send()),
                     (c_valid(way, t), lambda l=l, way=way, t=t: sib_out(l, c_in_chip(way, t)).wait_send()),
                 ])
         for m in range(cols // mt):

time: 160 us -> 157 us (0.981)
  Pallas kernels: 153 us -> 150 us
    pallas_call x1, Pallas kernels: 153 us -> 150 us  [shards(): pl.pallas_call(functools.partial(kernel, n, ns, tok, cols, ocols, mt), ou...]
where the time goes in v2:
time: 157 us
  Pallas kernels  150 us (96%)
  local copies, waits for them, and re-layouts  5.71 us (4%)
    pallas_call x1, Pallas kernels, shards(): pl.pallas_call(functools.partial(kernel, n, ns, tok, cols, ocols, mt), ou...  150 us
    unnamed x4, local copies, waits for them, and re-layouts  5.71 us

profile of v2, /device:TPU:0, one launch (start us, length us, event | category | flops | bytes accessed | tf_op | source)
XLA Modules:
  0.0 156.6 jit_solution(13722648407462891087)
XLA Ops:
  0.6 150.2 %shard_map.59 = (f32[1280,640]{1,0:T(8,128)}, f32[1280,640]{1,0:T(8,128)}) custom-call(bf16[256,1280]{1,0:T(8,128)(2,1)} %c1.1, bf16[256,1280]{1,0:T(8,128)(2,1)} %t1.1, bf16[256,1280]{1,0:T(8,128)(2,1)} %c2.1, bf16[256,1280]{1,0:T(8,128)(2,1)} %t2.1), custom_call_target="tpu_custom_call" | custom-call | flops 22817013760 | bytes 9175040 | tf_op jit(solution)/shard_map/pallas_call | solution.py:380
  150.8 0.0 copy-start
  150.9 4.0 %copy.8 = f32[1280,640]{1,0:T(8,128)} copy(f32[1280,640]{1,0:T(8,128)} %get-tuple-element.4) | data formatting | bytes 6553600
  154.8 0.0 copy-done
  154.8 1.7 %copy.9 = f32[1280,640]{1,0:T(8,128)} copy(f32[1280,640]{1,0:T(8,128)S(1)} %copy-done) | data formatting | bytes 6553600
Async XLA Ops:
  150.8 4.0 %copy-start = (f32[1280,640]{1,0:T(8,128)S(1)}, f32[1280,640]{1,0:T(8,128)}, u32[]{:S(2)}) copy-start(f32[1280,640]{1,0:T(8,128)} %get-tuple-element.5) | copy-start | bytes 9830404

commit v3 on v2

--- a/solution.py
+++ b/solution.py
@@ -53,7 +53,7 @@
     n, ns, tok, cols, ocols, mt,
     c1, t1, c2, t2, out1, out2,
     c_all, t_all, stage, t_scaled, obuf, acc, ar1, ar2, mine,
-    loc_sem, tl_sem, ta_send, ta_recv, tb_loc, tb_send, tb_recv, tc_send, tc_recv,
+    loc_sem, tl_sem, ta_send, ta_recv, tb_loc, tb_send, tb_recv, tc_send, tc_recv, ts_send, ts_recv,
     c_send, c_recv, sib_send, sib_recv, a1_send, a1_recv, a2_send, a2_recv, osem,
 ):
     nz = n // 2
@@ -110,23 +110,26 @@
                       ta_recv.at[l, q, h], r, q)
 
     def tb(l, j):
-        return remote(stage.at[l, j // 2, j % 2], t_all.at[l, r, quarter(s)],
+        return remote(stage.at[l, j // 2, j % 2], t_all.at[l, 0, r, quarter(s)],
                       tb_send.at[l, j], tb_recv.at[l, r], j, s)
 
     def tb_in(l, j):
-        return remote(stage.at[l, j // 2, j % 2], t_all.at[l, j, quarter(s)],
+        return remote(stage.at[l, j // 2, j % 2], t_all.at[l, 0, j, quarter(s)],
                       tb_send.at[l, j], tb_recv.at[l, j], j, s)
 
     def tb_own(l, j):
-        return pltpu.make_async_copy(stage.at[l, j // 2, j % 2], t_all.at[l, r, quarter(s)], tb_loc.at[l])
+        return pltpu.make_async_copy(stage.at[l, j // 2, j % 2], t_all.at[l, 0, r, quarter(s)], tb_loc.at[l])
 
     def tc(l, q):
-        part = t_all.at[l, :, quarter(s)]
+        part = t_all.at[l, 0, :, quarter(s)]
         return remote(part, part, tc_send.at[l, q], tc_recv.at[l, s], r, q)
 
     def tc_in(l, q):
-        part = t_all.at[l, :, quarter(q)]
+        part = t_all.at[l, 0, :, quarter(q)]
         return remote(part, part, tc_send.at[l, q], tc_recv.at[l, q], r, q)
+
+    def t_sib(l):
+        return remote(t_all.at[l, 0], t_all.at[l, 1], ts_send.at[l], ts_recv.at[l], sib, s)
 
     def c_copy(l, way, t):
         chip = z - t if way == 0 else z + t
@@ -205,40 +208,50 @@
         for q in range(ns):
             when_each([(q != s, lambda l=l, q=q: tc(l, q).start())])
 
-    def gram_block(l, i, j):
-        a = pl.ds(pl.multiple_of(i * 2 * tok, 2 * tok), 2 * tok)
-        b = pl.ds(pl.multiple_of(j * 2 * tok, 2 * tok), 2 * tok)
+    def gram_block(l, i, chip):
+        b = 2 * chip + core
+        pair = pl.ds(pl.multiple_of(i * 2 * tok, 2 * tok), 2 * tok)
         dims = (((1,), (1,)), ((), ()))
-        x = lax.dot_general(c_all[l, a, :], c_all[l, b, :], dims, preferred_element_type=F32)
-        ti = t_all[l, pl.ds(2 * i, 2)].reshape(2 * tok, ocols)
-        tj = t_all[l, pl.ds(2 * j, 2)].reshape(2 * tok, ocols)
-        y = lax.dot_general(ti, tj, dims, preferred_element_type=F32)
+        x = lax.dot_general(c_all[l, pair, :], c_all[l, rows(b), :], dims, preferred_element_type=F32)
+        y = jnp.zeros_like(x)
+        for h in range(2):
+            ti = t_all[l, h, pl.ds(2 * i, 2)].reshape(2 * tok, ocols)
+            y = y + lax.dot_general(ti, t_all[l, h, b], dims, preferred_element_type=F32)
         p = x * y
         for da in range(2):
+            a = 2 * i + da
+            share = jnp.where(jnp.logical_and(i == chip, a != b), 0.5, 1.0)
             part = jnp.sum(p[da * tok : (da + 1) * tok], axis=0, keepdims=True)
-            for db in range(2):
-                v = part[:, db * tok : db * tok + LANES]
-                for e in range(1, tok // LANES):
-                    v = v + part[:, db * tok + e * LANES : db * tok + (e + 1) * LANES]
-                acc[l, 2 * i + da, pl.ds(2 * j + db, 1), :] = v
-                acc[l, 2 * j + db, pl.ds(2 * i + da, 1), :] = v
+            v = part[:, :LANES]
+            for e in range(1, tok // LANES):
+                v = v + part[:, e * LANES : (e + 1) * LANES]
+            v = v * share
+            acc[l, a, pl.ds(b, 1), :] = v
+            acc[l, b, pl.ds(a, 1), :] = v
 
     def gram_step(l, t):
-        for way in range(2):
-            when_each([(c_valid(way, t), lambda l=l, way=way, t=t: sib_in(l, c_in_chip(way, t)).wait_recv())])
         lo0, hi0 = jnp.maximum(z - t, 0), jnp.minimum(z + t, nz - 1)
         lo1, hi1 = jnp.maximum(z - 1 - t, 0), jnp.minimum(z + 1 + t, nz - 1)
-        down = jnp.where(lo1 < lo0, hi0 - lo1 + 1, 0)
-        up = jnp.where(hi1 > hi0, hi1 - lo1 + 1, 0)
+        down = jnp.where(lo1 < lo0, 1, 0)
+        up = jnp.where(hi1 > hi0, 1, 0)
+        width = hi0 - lo0 + 1
         own = 1 if t == 0 else 0
 
-        def body(k, _):
-            i = jnp.where(k < own, z, jnp.where(k < own + down, lo1, lo1 + k - own - down))
-            j = jnp.where(k < own, z, jnp.where(k < own + down, lo1 + k - own, hi1))
-            gram_block(l, i, j)
+        def earlier(k, _):
+            first = k < down * width
+            gram_block(l, jnp.where(first, lo0 + k, lo0 + k - down * width), jnp.where(first, lo1, hi1))
             return 0
 
-        lax.fori_loop(0, own + down + up, body, 0)
+        def among(k, _):
+            i = jnp.where(k < own, z, jnp.where(k < own + down, lo1, jnp.where(k < own + down + up, hi1, lo1)))
+            chip = jnp.where(k < own, z, jnp.where(k < own + down, lo1, hi1))
+            gram_block(l, i, chip)
+            return 0
+
+        lax.fori_loop(0, (down + up) * width, earlier, 0)
+        for way in range(2):
+            when_each([(c_valid(way, t), lambda way=way: sib_in(l, c_in_chip(way, t)).wait_recv())])
+        lax.fori_loop(0, own + down + up + down * up, among, 0)
 
     def rows_sum_start(l):
         lane = lax.broadcasted_iota(jnp.int32, (n, LANES), 1)
@@ -277,53 +290,57 @@
         weights = replica_weights(gram, n) * (1.0 / float(tok))
         for rep in range(n):
             w = jnp.broadcast_to(weights[rep : rep + 1, :], (tok, ocols))
-            t_scaled[rep * tok : (rep + 1) * tok, :] = (t_all[l, rep].astype(F32) * w).astype(jnp.bfloat16)
+            t_scaled[rep * tok : (rep + 1) * tok, :] = (t_all[l, 0, rep].astype(F32) * w).astype(jnp.bfloat16)
 
         def body(m, _):
             part = pl.ds(pl.multiple_of(m * mt, mt), mt)
             obuf[l, part, :] = lax.dot_general(
                 c_all[l, :, part] if mt != cols else c_all[l],
                 t_scaled[...], (((0,), (0,)), ((), ())), preferred_element_type=F32,
-            )
+            ).astype(jnp.bfloat16)
             out_copy(l, m).start()
             return 0
 
         lax.fori_loop(0, cols // mt, body, 0)
 
     def inputs_ready(l):
+        for q in range(ns):
+            when_each([(q != s, lambda q=q: tc_in(l, q).wait_recv())])
+        t_sib(l).start()
         sib_in(l, z).wait_recv()
-        for q in range(ns):
-            when_each([(q != s, lambda q=q: tc_in(l, q).wait_recv())])
+        t_sib(l).wait_recv()
 
     last = nz - 2
+    at_end = jnp.logical_or(z == 0, z == nz - 1)
     ta_start(0)
     own_start(0)
-    ta_start(1)
+    acc[...] = jnp.zeros_like(acc)
     for copy in local:
         copy.wait()
     for l in layers:
         sib_out(l, z).start()
     tb_start(0)
+    ta_start(1)
+    tb_start(1)
     own_sent(0)
     own_start(1)
     arrive(0, 0)
-    tb_start(1)
     share_t(0)
+    share_t(1)
     for t in range(1, last):
         arrive(0, t)
         arrive(1, t - 1)
-        if t == 1:
-            share_t(1)
+    when_each([(jnp.logical_not(at_end), lambda: arrive(1, last - 1))])
     inputs_ready(0)
     for t in range(last):
         gram_step(0, t)
-    arrive(1, last - 1)
     arrive(0, last)
     gram_step(0, last)
     rows_sum_start(0)
     inputs_ready(1)
     gram_step(1, 0)
     replica_sum_start(0)
+    when_each([(at_end, lambda: arrive(1, last - 1))])
     for t in range(1, last):
         gram_step(1, t)
     finish(0)
@@ -349,6 +366,7 @@
 
             when_each([(j != r, drain_b)])
         sib_out(l, z).wait_send()
+        t_sib(l).wait_send()
         for t in range(nz - 1):
             for way in range(2):
                 when_each([
@@ -377,17 +395,17 @@
         bf = jnp.bfloat16
         any_spec = pl.BlockSpec(memory_space=pl.ANY)
         flops = LAYERS * 2 * n * tok * (cols * ocols + n * tok * (cols + ocols) // 2)
-        return pl.pallas_call(
+        combined = pl.pallas_call(
             functools.partial(kernel, n, ns, tok, cols, ocols, mt),
-            out_shape=[jax.ShapeDtypeStruct((cols, ocols), F32)] * 2,
+            out_shape=[jax.ShapeDtypeStruct((cols, ocols), bf)] * 2,
             in_specs=[any_spec] * 4,
             out_specs=[any_spec] * 2,
             scratch_shapes=[
                 pltpu.VMEM((LAYERS, n * tok, cols), bf),
-                pltpu.VMEM((LAYERS, n, tok, ocols), bf),
+                pltpu.VMEM((LAYERS, 2, n, tok, ocols), bf),
                 pltpu.VMEM((LAYERS, ns, 2, tok // ns, ocols), bf),
                 pltpu.VMEM((n * tok, ocols), bf),
-                pltpu.VMEM((LAYERS, cols, ocols), F32),
+                pltpu.VMEM((LAYERS, cols, ocols), bf),
                 pltpu.VMEM((LAYERS, n, n, LANES), F32),
                 pltpu.VMEM((LAYERS, ns, n, LANES), F32),
                 pltpu.VMEM((LAYERS, n, n, LANES), F32),
@@ -395,7 +413,7 @@
                 dma(LAYERS), dma(LAYERS, 2),
                 dma(LAYERS, ns, 2), dma(LAYERS, ns, 2),
                 dma(LAYERS), dma(LAYERS, n), dma(LAYERS, n),
-                dma(LAYERS, ns), dma(LAYERS, ns),
+                dma(LAYERS, ns), dma(LAYERS, ns), dma(LAYERS), dma(LAYERS),
                 dma(LAYERS, 2, nz), dma(LAYERS, 2, nz),
                 dma(LAYERS, nz), dma(LAYERS, nz),
                 dma(LAYERS, ns), dma(LAYERS, ns),
@@ -407,9 +425,10 @@
             ),
             cost_estimate=pl.CostEstimate(
                 flops=flops, transcendentals=0,
-                bytes_accessed=LAYERS * (2 * tok * cols * 2 + cols * ocols * 4),
+                bytes_accessed=LAYERS * (2 * tok * cols * 2 + cols * ocols * 2),
             ),
         )(context_one, halves(cotangent_one), context_two, halves(cotangent_two))
+        return tuple(value.astype(F32) for value in combined)
 
     return jax.shard_map(
         shards,

time: 157 us -> 154 us (0.981)
  local copies, waits for them, and re-layouts: 5.71 us -> 0.01 us
  other arithmetic: 0 us -> 5.39 us
  Pallas kernels: 150 us -> 148 us
    unnamed x4 -> x2, local copies, waits for them, and re-layouts: 5.71 us -> 0.01 us
    convert_element_type x0 -> x2, other arithmetic: none -> 5.39 us  [shards(): return tuple((value.astype(F32) for value in combined))]
    pallas_call x1, Pallas kernels: 150 us -> 148 us  [shards(): pl.pallas_call(functools.partial(kernel, n, ns, tok, cols, ocols, mt), ou...]
where the time goes in v3:
time: 154 us
  Pallas kernels  148 us (96%)
  other arithmetic  5.39 us (4%)
    pallas_call x1, Pallas kernels, shards(): pl.pallas_call(functools.partial(kernel, n, ns, tok, cols, ocols, mt), ou...  148 us
    convert_element_type x2, other arithmetic, shards(): return tuple((value.astype(F32) for value in combined))  5.39 us

profile of v3, /device:TPU:0, one launch (start us, length us, event | category | flops | bytes accessed | tf_op | source)
XLA Modules:
  0.0 154.1 jit_solution(741792710733585971)
XLA Ops:
  0.6 148.1 %shard_map.59 = (bf16[1280,640]{1,0:T(8,128)(2,1)}, bf16[1280,640]{1,0:T(8,128)(2,1)}) custom-call(bf16[256,1280]{1,0:T(8,128)(2,1)} %c1.1, bf16[256,1280]{1,0:T(8,128)(2,1)} %t1.1, bf16[256,1280]{1,0:T(8,128)(2,1)} %c2.1, bf16[256,1280]{1,0:T(8,128)(2,1)} %t2.1), custom_call_target="tpu_custom_call" | custom-call | flops 22817013760 | bytes 5898240 | tf_op jit(solution)/shard_map/pallas_call | solution.py:398
  148.7 0.0 copy-start
  148.7 3.5 %convert_element_type.6 = f32[1280,640]{1,0:T(8,128)} convert(bf16[1280,640]{1,0:T(8,128)(2,1)} %get-tuple-element.4) | non-fusion elementwise | flops 819200 | bytes 4915200 | tf_op jit(solution)/shard_map/convert_element_type | solution.py:431
  152.2 0.0 copy-done
  152.2 1.9 %convert_element_type.7 = f32[1280,640]{1,0:T(8,128)} convert(bf16[1280,640]{1,0:T(8,128)(2,1)S(1)} %copy-done) | non-fusion elementwise | flops 819200 | bytes 4915200 | tf_op jit(solution)/shard_map/convert_element_type | solution.py:431
Async XLA Ops:
  148.7 3.5 %copy-start = (bf16[1280,640]{1,0:T(8,128)(2,1)S(1)}, bf16[1280,640]{1,0:T(8,128)(2,1)}, u32[]{:S(2)}) copy-start(bf16[1280,640]{1,0:T(8,128)(2,1)} %get-tuple-element.5) | copy-start | bytes 4915204

commit v4 on v3

--- a/solution.py
+++ b/solution.py
@@ -120,16 +120,17 @@
     def tb_own(l, j):
         return pltpu.make_async_copy(stage.at[l, j // 2, j % 2], t_all.at[l, 0, r, quarter(s)], tb_loc.at[l])
 
-    def tc(l, q):
-        part = t_all.at[l, 0, :, quarter(s)]
-        return remote(part, part, tc_send.at[l, q], tc_recv.at[l, s], r, q)
-
-    def tc_in(l, q):
-        part = t_all.at[l, 0, :, quarter(q)]
-        return remote(part, part, tc_send.at[l, q], tc_recv.at[l, q], r, q)
-
-    def t_sib(l):
-        return remote(t_all.at[l, 0], t_all.at[l, 1], ts_send.at[l], ts_recv.at[l], sib, s)
+    def tc(l, q, chip):
+        part = t_all.at[l, 0, pl.ds(2 * chip, 2), quarter(s)]
+        return remote(part, part, tc_send.at[l, q, chip], tc_recv.at[l, s, chip], r, q)
+
+    def tc_in(l, q, chip):
+        part = t_all.at[l, 0, pl.ds(2 * chip, 2), quarter(q)]
+        return remote(part, part, tc_send.at[l, q, chip], tc_recv.at[l, q, chip], r, q)
+
+    def t_sib(l, q):
+        return remote(t_all.at[l, 0, :, quarter(q)], t_all.at[l, 1, :, quarter(q)],
+                      ts_send.at[l, q], ts_recv.at[l, q], sib, s)
 
     def c_copy(l, way, t):
         chip = z - t if way == 0 else z + t
@@ -200,13 +201,17 @@
             when_each([(c_valid(way, t), take)])
 
     def share_t(l):
-        for j in range(n):
-            when_each([
-                (j != r, lambda l=l, j=j: tb_in(l, j).wait_recv()),
-                (j == r, lambda l=l, j=j: tb_own(l, j).wait()),
-            ])
-        for q in range(ns):
-            when_each([(q != s, lambda l=l, q=q: tc(l, q).start())])
+        for k in range(nz):
+            chip = lax.rem(z + k, nz)
+            if k == 0:
+                tb_own(l, r).wait()
+                tb_in(l, sib).wait_recv()
+            else:
+                tb_in(l, 2 * chip).wait_recv()
+                tb_in(l, 2 * chip + 1).wait_recv()
+            for q in range(ns):
+                when_each([(q != s, lambda q=q, chip=chip: tc(l, q, chip).start())])
+        t_sib(l, s).start()
 
     def gram_block(l, i, chip):
         b = 2 * chip + core
@@ -305,10 +310,15 @@
 
     def inputs_ready(l):
         for q in range(ns):
-            when_each([(q != s, lambda q=q: tc_in(l, q).wait_recv())])
-        t_sib(l).start()
+            def pass_on(q=q):
+                for chip in range(nz):
+                    tc_in(l, q, chip).wait_recv()
+                t_sib(l, q).start()
+
+            when_each([(q != s, pass_on)])
         sib_in(l, z).wait_recv()
-        t_sib(l).wait_recv()
+        for q in range(ns):
+            t_sib(l, q).wait_recv()
 
     last = nz - 2
     at_end = jnp.logical_or(z == 0, z == nz - 1)
@@ -321,11 +331,11 @@
         sib_out(l, z).start()
     tb_start(0)
     ta_start(1)
+    share_t(0)
     tb_start(1)
     own_sent(0)
     own_start(1)
     arrive(0, 0)
-    share_t(0)
     share_t(1)
     for t in range(1, last):
         arrive(0, t)
@@ -355,7 +365,8 @@
             def drain(l=l, q=q):
                 for h in range(2):
                     ta(l, q, h).wait_send()
-                tc(l, q).wait_send()
+                for chip in range(nz):
+                    tc(l, q, chip).wait_send()
                 remote(mine.at[l, 0], ar1.at[l, s], a1_send.at[l, q], a1_recv.at[l, s], r, q).wait_send()
 
             when_each([(q != s, drain)])
@@ -366,7 +377,8 @@
 
             when_each([(j != r, drain_b)])
         sib_out(l, z).wait_send()
-        t_sib(l).wait_send()
+        for q in range(ns):
+            t_sib(l, q).wait_send()
         for t in range(nz - 1):
             for way in range(2):
                 when_each([
@@ -413,7 +425,7 @@
                 dma(LAYERS), dma(LAYERS, 2),
                 dma(LAYERS, ns, 2), dma(LAYERS, ns, 2),
                 dma(LAYERS), dma(LAYERS, n), dma(LAYERS, n),
-                dma(LAYERS, ns), dma(LAYERS, ns), dma(LAYERS), dma(LAYERS),
+                dma(LAYERS, ns, nz), dma(LAYERS, ns, nz), dma(LAYERS, ns), dma(LAYERS, ns),
                 dma(LAYERS, 2, nz), dma(LAYERS, 2, nz),
                 dma(LAYERS, nz), dma(LAYERS, nz),
                 dma(LAYERS, ns), dma(LAYERS, ns),

time: 154 us -> 156 us (1.013)
  Pallas kernels: 148 us -> 150 us
    pallas_call x1, Pallas kernels: 148 us -> 150 us  [shards(): pl.pallas_call(functools.partial(kernel, n, ns, tok, cols, ocols, mt), ou...]
where the time goes in v4:
time: 156 us
  Pallas kernels  150 us (96%)
  other arithmetic  5.39 us (3%)
    pallas_call x1, Pallas kernels, shards(): pl.pallas_call(functools.partial(kernel, n, ns, tok, cols, ocols, mt), ou...  150 us
    convert_element_type x2, other arithmetic, shards(): return tuple((value.astype(F32) for value in combined))  5.39 us

profile of v4, /device:TPU:0, one launch (start us, length us, event | category | flops | bytes accessed | tf_op | source)
XLA Modules:
  0.0 155.8 jit_solution(10872009907322074838)
XLA Ops:
  0.6 149.8 %shard_map.59 = (bf16[1280,640]{1,0:T(8,128)(2,1)}, bf16[1280,640]{1,0:T(8,128)(2,1)}) custom-call(bf16[256,1280]{1,0:T(8,128)(2,1)} %c1.1, bf16[256,1280]{1,0:T(8,128)(2,1)} %t1.1, bf16[256,1280]{1,0:T(8,128)(2,1)} %c2.1, bf16[256,1280]{1,0:T(8,128)(2,1)} %t2.1), custom_call_target="tpu_custom_call" | custom-call | flops 22817013760 | bytes 5898240 | tf_op jit(solution)/shard_map/pallas_call | solution.py:410
  150.4 0.0 copy-start
  150.4 3.5 %convert_element_type.6 = f32[1280,640]{1,0:T(8,128)} convert(bf16[1280,640]{1,0:T(8,128)(2,1)} %get-tuple-element.4) | non-fusion elementwise | flops 819200 | bytes 4915200 | tf_op jit(solution)/shard_map/convert_element_type | solution.py:443
  153.9 0.0 copy-done
  153.9 1.9 %convert_element_type.7 = f32[1280,640]{1,0:T(8,128)} convert(bf16[1280,640]{1,0:T(8,128)(2,1)S(1)} %copy-done) | non-fusion elementwise | flops 819200 | bytes 4915200 | tf_op jit(solution)/shard_map/convert_element_type | solution.py:443
Async XLA Ops:
  150.4 3.5 %copy-start = (bf16[1280,640]{1,0:T(8,128)(2,1)S(1)}, bf16[1280,640]{1,0:T(8,128)(2,1)}, u32[]{:S(2)}) copy-start(bf16[1280,640]{1,0:T(8,128)(2,1)} %get-tuple-element.5) | copy-start | bytes 4915204

commit v5 on v4

--- a/solution.py
+++ b/solution.py
@@ -52,7 +52,7 @@
 def kernel(
     n, ns, tok, cols, ocols, mt,
     c1, t1, c2, t2, out1, out2,
-    c_all, t_all, stage, t_scaled, obuf, acc, ar1, ar2, mine,
+    c_all, ct_all, t_all, stage, t_scaled, obuf, acc, ar1, ar2, mine,
     loc_sem, tl_sem, ta_send, ta_recv, tb_loc, tb_send, tb_recv, tc_send, tc_recv, ts_send, ts_recv,
     c_send, c_recv, sib_send, sib_recv, a1_send, a1_recv, a2_send, a2_recv, osem,
 ):
@@ -175,10 +175,6 @@
     def own_start(l):
         for way in range(2):
             when_each([(c_sends(way, 0), lambda way=way: c_copy(l, way, 0).start())])
-
-    def own_sent(l):
-        for way in range(2):
-            when_each([(c_sends(way, 0), lambda way=way: c_copy(l, way, 0).wait_send())])
 
     def tb_start(l):
         for q in range(ns):
@@ -258,6 +254,19 @@
             when_each([(c_valid(way, t), lambda way=way: sib_in(l, c_in_chip(way, t)).wait_recv())])
         lax.fori_loop(0, own + down + up + down * up, among, 0)
 
+    def turn(l, t):
+        down = jnp.where(c_valid(0, t), 1, 0)
+        up = jnp.where(c_valid(1, t), 1, 0)
+        own = 1 if t == 0 else 0
+
+        def body(k, _):
+            chip = jnp.where(k < own, z, jnp.where(k < own + down, z - 1 - t, z + 1 + t))
+            pair = pl.ds(pl.multiple_of(chip * 2 * tok, 2 * tok), 2 * tok)
+            ct_all[l, :, pair] = c_all[l, pair, :].T
+            return 0
+
+        lax.fori_loop(0, own + down + up, body, 0)
+
     def rows_sum_start(l):
         lane = lax.broadcasted_iota(jnp.int32, (n, LANES), 1)
         value = jnp.zeros((n, LANES), F32)
@@ -300,8 +309,8 @@
         def body(m, _):
             part = pl.ds(pl.multiple_of(m * mt, mt), mt)
             obuf[l, part, :] = lax.dot_general(
-                c_all[l, :, part] if mt != cols else c_all[l],
-                t_scaled[...], (((0,), (0,)), ((), ())), preferred_element_type=F32,
+                ct_all[l, part, :], t_scaled[...], (((1,), (0,)), ((), ())),
+                preferred_element_type=F32,
             ).astype(jnp.bfloat16)
             out_copy(l, m).start()
             return 0
@@ -331,32 +340,37 @@
         sib_out(l, z).start()
     tb_start(0)
     ta_start(1)
+    arrive(0, 0)
     share_t(0)
     tb_start(1)
-    own_sent(0)
-    own_start(1)
-    arrive(0, 0)
-    share_t(1)
     for t in range(1, last):
         arrive(0, t)
-        arrive(1, t - 1)
+    own_start(1)
+    share_t(1)
+    for t in range(last - 1):
+        arrive(1, t)
     when_each([(jnp.logical_not(at_end), lambda: arrive(1, last - 1))])
     inputs_ready(0)
     for t in range(last):
         gram_step(0, t)
+        turn(0, t)
     arrive(0, last)
     gram_step(0, last)
     rows_sum_start(0)
+    turn(0, last)
     inputs_ready(1)
     gram_step(1, 0)
     replica_sum_start(0)
+    turn(1, 0)
+    finish(0)
     when_each([(at_end, lambda: arrive(1, last - 1))])
     for t in range(1, last):
         gram_step(1, t)
-    finish(0)
+        turn(1, t)
     arrive(1, last)
     gram_step(1, last)
     rows_sum_start(1)
+    turn(1, last)
     replica_sum_start(1)
     finish(1)
 
@@ -382,7 +396,7 @@
         for t in range(nz - 1):
             for way in range(2):
                 when_each([
-                    (jnp.logical_and(c_sends(way, t), l + t > 0), lambda l=l, way=way, t=t: c_copy(l, way, t).wait_send()),
+                    (c_sends(way, t), lambda l=l, way=way, t=t: c_copy(l, way, t).wait_send()),
                     (c_valid(way, t), lambda l=l, way=way, t=t: sib_out(l, c_in_chip(way, t)).wait_send()),
                 ])
         for m in range(cols // mt):
@@ -414,6 +428,7 @@
             out_specs=[any_spec] * 2,
             scratch_shapes=[
                 pltpu.VMEM((LAYERS, n * tok, cols), bf),
+                pltpu.VMEM((LAYERS, cols, n * tok), bf),
                 pltpu.VMEM((LAYERS, 2, n, tok, ocols), bf),
                 pltpu.VMEM((LAYERS, ns, 2, tok // ns, ocols), bf),
                 pltpu.VMEM((n * tok, ocols), bf),

time: 156 us -> 158 us (1.013)
    pallas_call x1, Pallas kernels: 150 us -> 151 us  [shards(): pl.pallas_call(functools.partial(kernel, n, ns, tok, cols, ocols, mt), ou...]
where the time goes in v5:
time: 158 us; the launch traced here: 157 us
  Pallas kernels  151 us (96%)
  other arithmetic  5.39 us (3%)
    pallas_call x1, Pallas kernels, shards(): pl.pallas_call(functools.partial(kernel, n, ns, tok, cols, ocols, mt), ou...  151 us
    convert_element_type x2, other arithmetic, shards(): return tuple((value.astype(F32) for value in combined))  5.39 us

profile of v5, /device:TPU:0, one launch (start us, length us, event | category | flops | bytes accessed | tf_op | source)
XLA Modules:
  0.0 157.5 jit_solution(1377257340834249886)
XLA Ops:
  0.6 151.4 %shard_map.59 = (bf16[1280,640]{1,0:T(8,128)(2,1)}, bf16[1280,640]{1,0:T(8,128)(2,1)}) custom-call(bf16[256,1280]{1,0:T(8,128)(2,1)} %c1.1, bf16[256,1280]{1,0:T(8,128)(2,1)} %t1.1, bf16[256,1280]{1,0:T(8,128)(2,1)} %c2.1, bf16[256,1280]{1,0:T(8,128)(2,1)} %t2.1), custom_call_target="tpu_custom_call" | custom-call | flops 22817013760 | bytes 5898240 | tf_op jit(solution)/shard_map/pallas_call | solution.py:424
  152.1 0.0 copy-start
  152.1 3.5 %convert_element_type.6 = f32[1280,640]{1,0:T(8,128)} convert(bf16[1280,640]{1,0:T(8,128)(2,1)} %get-tuple-element.4) | non-fusion elementwise | flops 819200 | bytes 4915200 | tf_op jit(solution)/shard_map/convert_element_type | solution.py:458
  155.6 0.0 copy-done
  155.6 1.9 %convert_element_type.7 = f32[1280,640]{1,0:T(8,128)} convert(bf16[1280,640]{1,0:T(8,128)(2,1)S(1)} %copy-done) | non-fusion elementwise | flops 819200 | bytes 4915200 | tf_op jit(solution)/shard_map/convert_element_type | solution.py:458
Async XLA Ops:
  152.1 3.5 %copy-start = (bf16[1280,640]{1,0:T(8,128)(2,1)S(1)}, bf16[1280,640]{1,0:T(8,128)(2,1)}, u32[]{:S(2)}) copy-start(bf16[1280,640]{1,0:T(8,128)(2,1)} %get-tuple-element.5) | copy-start | bytes 4915204

commit v6 on v5

--- a/solution.py
+++ b/solution.py
@@ -132,12 +132,16 @@
         return remote(t_all.at[l, 0, :, quarter(q)], t_all.at[l, 1, :, quarter(q)],
                       ts_send.at[l, q], ts_recv.at[l, q], sib, s)
 
-    def c_copy(l, way, t):
+    def half_rows(rep, half):
+        start = pl.multiple_of(rep * tok + half * (tok // 2), tok // 2)
+        return pl.ds(start, tok // 2)
+
+    def c_copy(l, way, t, half):
         chip = z - t if way == 0 else z + t
-        block = c_all.at[l, rows(2 * chip + core)]
-        src = c_in[l] if t == 0 else block
+        block = c_all.at[l, half_rows(2 * chip + core, half)]
+        src = c_in[l].at[pl.ds(half * (tok // 2), tok // 2)] if t == 0 else block
         to = r + 2 if way == 0 else r - 2
-        return remote(src, block, c_send.at[l, way, t], c_recv.at[l, way, t], to, s)
+        return remote(src, block, c_send.at[l, way, t, half], c_recv.at[l, way, t, half], to, s)
 
     def c_sends(way, t):
         if way == 0:
@@ -151,9 +155,9 @@
         chip = c_in_chip(way, t)
         return chip >= 0 if way == 0 else chip <= nz - 1
 
-    def c_wait(l, way, t):
-        block = c_all.at[l, rows(2 * c_in_chip(way, t) + core)]
-        remote(block, block, c_send.at[l, way, t], c_recv.at[l, way, t], sib, s).wait_recv()
+    def c_wait(l, way, t, half):
+        block = c_all.at[l, half_rows(2 * c_in_chip(way, t) + core, half)]
+        remote(block, block, c_send.at[l, way, t, half], c_recv.at[l, way, t, half], sib, s).wait_recv()
 
     def sib_out(l, chip):
         block = c_all.at[l, rows(2 * chip + core)]
@@ -174,7 +178,8 @@
 
     def own_start(l):
         for way in range(2):
-            when_each([(c_sends(way, 0), lambda way=way: c_copy(l, way, 0).start())])
+            for half in range(2):
+                when_each([(c_sends(way, 0), lambda way=way, half=half: c_copy(l, way, 0, half).start())])
 
     def tb_start(l):
         for q in range(ns):
@@ -187,14 +192,16 @@
             ])
 
     def arrive(l, t):
-        for way in range(2):
-            def take(l=l, way=way, t=t):
-                c_wait(l, way, t)
-                if t + 1 <= nz - 2:
-                    when_each([(c_sends(way, t + 1), lambda: c_copy(l, way, t + 1).start())])
-                sib_out(l, c_in_chip(way, t)).start()
-
-            when_each([(c_valid(way, t), take)])
+        for half in range(2):
+            for way in range(2):
+                def take(way=way, half=half):
+                    c_wait(l, way, t, half)
+                    if t + 1 <= nz - 2:
+                        when_each([(c_sends(way, t + 1), lambda: c_copy(l, way, t + 1, half).start())])
+                    if half == 1:
+                        sib_out(l, c_in_chip(way, t)).start()
+
+                when_each([(c_valid(way, t), take)])
 
     def share_t(l):
         for k in range(nz):
@@ -340,37 +347,37 @@
         sib_out(l, z).start()
     tb_start(0)
     ta_start(1)
+    own_start(1)
     arrive(0, 0)
+    tb_start(1)
+    arrive(1, 0)
     share_t(0)
-    tb_start(1)
     for t in range(1, last):
         arrive(0, t)
-    own_start(1)
-    share_t(1)
-    for t in range(last - 1):
-        arrive(1, t)
+        if t == 1:
+            share_t(1)
+        if t < last - 1:
+            arrive(1, t)
     when_each([(jnp.logical_not(at_end), lambda: arrive(1, last - 1))])
     inputs_ready(0)
     for t in range(last):
         gram_step(0, t)
         turn(0, t)
+    when_each([(at_end, lambda: arrive(1, last - 1))])
+    inputs_ready(1)
+    for t in range(last):
+        gram_step(1, t)
+        turn(1, t)
     arrive(0, last)
     gram_step(0, last)
     rows_sum_start(0)
     turn(0, last)
-    inputs_ready(1)
-    gram_step(1, 0)
     replica_sum_start(0)
-    turn(1, 0)
-    finish(0)
-    when_each([(at_end, lambda: arrive(1, last - 1))])
-    for t in range(1, last):
-        gram_step(1, t)
-        turn(1, t)
     arrive(1, last)
     gram_step(1, last)
     rows_sum_start(1)
     turn(1, last)
+    finish(0)
     replica_sum_start(1)
     finish(1)
 
@@ -395,8 +402,9 @@
             t_sib(l, q).wait_send()
         for t in range(nz - 1):
             for way in range(2):
+                for half in range(2):
+                    when_each([(c_sends(way, t), lambda l=l, way=way, t=t, half=half: c_copy(l, way, t, half).wait_send())])
                 when_each([
-                    (c_sends(way, t), lambda l=l, way=way, t=t: c_copy(l, way, t).wait_send()),
                     (c_valid(way, t), lambda l=l, way=way, t=t: sib_out(l, c_in_chip(way, t)).wait_send()),
                 ])
         for m in range(cols // mt):
@@ -441,7 +449,7 @@
                 dma(LAYERS, ns, 2), dma(LAYERS, ns, 2),
                 dma(LAYERS), dma(LAYERS, n), dma(LAYERS, n),
                 dma(LAYERS, ns, nz), dma(LAYERS, ns, nz), dma(LAYERS, ns), dma(LAYERS, ns),
-                dma(LAYERS, 2, nz), dma(LAYERS, 2, nz),
+                dma(LAYERS, 2, nz, 2), dma(LAYERS, 2, nz, 2),
                 dma(LAYERS, nz), dma(LAYERS, nz),
                 dma(LAYERS, ns), dma(LAYERS, ns),
                 dma(LAYERS, n), dma(LAYERS, n),

time: 158 us -> 159 us (level)
  Pallas kernels: 151 us -> 153 us
where the time goes in v6:
time: 159 us
  Pallas kernels  153 us (96%)
  other arithmetic  5.39 us (3%)
    pallas_call x1, Pallas kernels, shards(): pl.pallas_call(functools.partial(kernel, n, ns, tok, cols, ocols, mt), ou...  153 us
    convert_element_type x2, other arithmetic, shards(): return tuple((value.astype(F32) for value in combined))  5.39 us

profile of v6, /device:TPU:0, one launch (start us, length us, event | category | flops | bytes accessed | tf_op | source)
XLA Modules:
  0.0 158.5 jit_solution(11810101848011842746)
XLA Ops:
  0.6 152.5 %shard_map.59 = (bf16[1280,640]{1,0:T(8,128)(2,1)}, bf16[1280,640]{1,0:T(8,128)(2,1)}) custom-call(bf16[256,1280]{1,0:T(8,128)(2,1)} %c1.1, bf16[256,1280]{1,0:T(8,128)(2,1)} %t1.1, bf16[256,1280]{1,0:T(8,128)(2,1)} %c2.1, bf16[256,1280]{1,0:T(8,128)(2,1)} %t2.1), custom_call_target="tpu_custom_call" | custom-call | flops 22817013760 | bytes 5898240 | tf_op jit(solution)/shard_map/pallas_call | solution.py:432
  153.1 0.0 copy-start
  153.2 3.5 %convert_element_type.6 = f32[1280,640]{1,0:T(8,128)} convert(bf16[1280,640]{1,0:T(8,128)(2,1)} %get-tuple-element.4) | non-fusion elementwise | flops 819200 | bytes 4915200 | tf_op jit(solution)/shard_map/convert_element_type | solution.py:466
  156.6 0.0 copy-done
  156.6 1.9 %convert_element_type.7 = f32[1280,640]{1,0:T(8,128)} convert(bf16[1280,640]{1,0:T(8,128)(2,1)S(1)} %copy-done) | non-fusion elementwise | flops 819200 | bytes 4915200 | tf_op jit(solution)/shard_map/convert_element_type | solution.py:466
Async XLA Ops:
  153.1 3.5 %copy-start = (bf16[1280,640]{1,0:T(8,128)(2,1)S(1)}, bf16[1280,640]{1,0:T(8,128)(2,1)}, u32[]{:S(2)}) copy-start(bf16[1280,640]{1,0:T(8,128)(2,1)} %get-tuple-element.5) | copy-start | bytes 4915204

commit v7 on v3

--- a/solution.py
+++ b/solution.py
@@ -174,10 +174,6 @@
     def own_start(l):
         for way in range(2):
             when_each([(c_sends(way, 0), lambda way=way: c_copy(l, way, 0).start())])
-
-    def own_sent(l):
-        for way in range(2):
-            when_each([(c_sends(way, 0), lambda way=way: c_copy(l, way, 0).wait_send())])
 
     def tb_start(l):
         for q in range(ns):
@@ -314,22 +310,24 @@
     at_end = jnp.logical_or(z == 0, z == nz - 1)
     ta_start(0)
     own_start(0)
+    ta_start(1)
+    own_start(1)
     acc[...] = jnp.zeros_like(acc)
     for copy in local:
         copy.wait()
     for l in layers:
         sib_out(l, z).start()
     tb_start(0)
-    ta_start(1)
     tb_start(1)
-    own_sent(0)
-    own_start(1)
     arrive(0, 0)
     share_t(0)
+    if last > 1:
+        arrive(1, 0)
     share_t(1)
     for t in range(1, last):
         arrive(0, t)
-        arrive(1, t - 1)
+        if t < last - 1:
+            arrive(1, t)
     when_each([(jnp.logical_not(at_end), lambda: arrive(1, last - 1))])
     inputs_ready(0)
     for t in range(last):
@@ -370,7 +368,7 @@
         for t in range(nz - 1):
             for way in range(2):
                 when_each([
-                    (jnp.logical_and(c_sends(way, t), l + t > 0), lambda l=l, way=way, t=t: c_copy(l, way, t).wait_send()),
+                    (c_sends(way, t), lambda l=l, way=way, t=t: c_copy(l, way, t).wait_send()),
                     (c_valid(way, t), lambda l=l, way=way, t=t: sib_out(l, c_in_chip(way, t)).wait_send()),
                 ])
         for m in range(cols // mt):

time: 154 us -> 159 us (1.032)
  Pallas kernels: 148 us -> 153 us
    pallas_call x1, Pallas kernels: 148 us -> 153 us  [shards(): pl.pallas_call(functools.partial(kernel, n, ns, tok, cols, ocols, mt), ou...]
where the time goes in v7:
time: 159 us
  Pallas kernels  153 us (96%)
  other arithmetic  5.39 us (3%)
    pallas_call x1, Pallas kernels, shards(): pl.pallas_call(functools.partial(kernel, n, ns, tok, cols, ocols, mt), ou...  153 us
    convert_element_type x2, other arithmetic, shards(): return tuple((value.astype(F32) for value in combined))  5.39 us

profile of v7, /device:TPU:0, one launch (start us, length us, event | category | flops | bytes accessed | tf_op | source)
XLA Modules:
  0.0 159.2 jit_solution(9116810416207323155)
XLA Ops:
  0.6 153.2 %shard_map.59 = (bf16[1280,640]{1,0:T(8,128)(2,1)}, bf16[1280,640]{1,0:T(8,128)(2,1)}) custom-call(bf16[256,1280]{1,0:T(8,128)(2,1)} %c1.1, bf16[256,1280]{1,0:T(8,128)(2,1)} %t1.1, bf16[256,1280]{1,0:T(8,128)(2,1)} %c2.1, bf16[256,1280]{1,0:T(8,128)(2,1)} %t2.1), custom_call_target="tpu_custom_call" | custom-call | flops 22817013760 | bytes 5898240 | tf_op jit(solution)/shard_map/pallas_call | solution.py:396
  153.8 0.0 copy-start
  153.8 3.5 %convert_element_type.6 = f32[1280,640]{1,0:T(8,128)} convert(bf16[1280,640]{1,0:T(8,128)(2,1)} %get-tuple-element.4) | non-fusion elementwise | flops 819200 | bytes 4915200 | tf_op jit(solution)/shard_map/convert_element_type | solution.py:429
  157.3 0.0 copy-done
  157.3 1.9 %convert_element_type.7 = f32[1280,640]{1,0:T(8,128)} convert(bf16[1280,640]{1,0:T(8,128)(2,1)S(1)} %copy-done) | non-fusion elementwise | flops 819200 | bytes 4915200 | tf_op jit(solution)/shard_map/convert_element_type | solution.py:429
Async XLA Ops:
  153.8 3.5 %copy-start = (bf16[1280,640]{1,0:T(8,128)(2,1)S(1)}, bf16[1280,640]{1,0:T(8,128)(2,1)}, u32[]{:S(2)}) copy-start(bf16[1280,640]{1,0:T(8,128)(2,1)} %get-tuple-element.5) | copy-start | bytes 4915204
